TPU v7x, 512 devices: a whole 4x4x16 slice. The times are simulated.
512 devices in a mesh: dp: 32 (over x_lo, z), cls: 16 (over x_hi, y, core).
Axes of the slice: x: 4 (x_hi: 2, x_lo: 2; x = x_hi * 2 + x_lo), y: 4, z: 16, core: 2. Of those that a mesh axis runs over, the one named last changes fastest.
Arguments:
- images: bfloat16 [2560, 2, 48, 256], P('dp'), may hold values from -420 to 420
- references: bfloat16 [256, 2, 48, 256], P('cls'), may hold values from -0.12 to 0.12
- ctf_rows: float32 [64, 48], replicated, may hold values from 0.2 to 1
- group_ids: int32 [2560], P('dp'), may hold values from 0 to 63
- noise_var: float32 [48], replicated, may hold values from 0.5 to 2
- class_prior: float32 [256], P('cls'), may hold values from 0.5 to 2
Outputs:
- new_references: float32 [256, 24576], P('cls', 'dp')
- occupancy: float32 [256], P('cls')
- log_evidence: float32 [2560], P('dp')
All inputs are finite; a program needn't handle non-finite values.
Results may differ from a plain program's by a relative error of at most 0.0071.
Values sent between devices are 32-bit elements; how exact they have to be, the bound alone decides.
A program may use at most 64 MiB of HBM per device.

v0:
```python
import math

import jax
import jax.numpy as jnp
from jax import lax
from jax.sharding import PartitionSpec as P

ROT = 36


def rotation_table(harmonics, rotations):
    product = (
        jnp.arange(harmonics, dtype=jnp.int32)[:, None]
        * jnp.arange(rotations, dtype=jnp.int32)[None, :]
        % rotations
    )
    angle = product.astype(jnp.float32) * (2.0 * math.pi / rotations)
    return jnp.concatenate([jnp.cos(angle), jnp.sin(angle)], axis=0)


def shards(images, references, ctf_rows, group_ids, noise_var, class_prior):
    hp = lax.Precision.HIGHEST
    img_count = images.shape[0]
    cycle_total = references.shape[2]
    harmonics = references.shape[3]
    class_count = references.shape[0]
    group_count = ctf_rows.shape[0]
    table = rotation_table(harmonics, ROT)
    onehot = (group_ids[:, None] == jnp.arange(group_count, dtype=jnp.int32)[None, :]).astype(
        jnp.float32
    )
    ctf = jnp.dot(onehot, ctf_rows, precision=hp)
    weight = ctf / noise_var[None, :]
    power_weight = ctf * ctf / noise_var[None, :]
    weighted = (images.astype(jnp.float32) * weight[:, None, :, None]).astype(jnp.bfloat16)
    swapped = jnp.stack([references[:, 1], -references[:, 0]], axis=1)
    stacked = jnp.stack([references, swapped], axis=1)
    cross = jnp.einsum("iprm,cqprm->icqm", weighted, stacked, preferred_element_type=jnp.float32)
    correlation = jnp.dot(cross.reshape(-1, 2 * harmonics), table, precision=hp).reshape(
        img_count, class_count, ROT
    )
    refs32 = references.astype(jnp.float32)
    cycle_power = jnp.sum(refs32 * refs32, axis=(1, 3))
    model_power = jnp.dot(power_weight, cycle_power.T, precision=hp)
    score = correlation - 0.5 * model_power[:, :, None] + jnp.log(class_prior)[None, :, None]
    local_peak = jnp.max(score, axis=(1, 2))
    peak = lax.pmax(local_peak, "cls")
    total = lax.psum(jnp.sum(jnp.exp(score - peak[:, None, None]), axis=(1, 2)), "cls")
    evidence = peak + jnp.log(total)
    posterior = jnp.exp(score - evidence[:, None, None])
    back = jnp.dot(posterior.reshape(-1, ROT), table.T, precision=hp).reshape(
        img_count, class_count, 2, harmonics
    )
    back = back.astype(jnp.bfloat16)
    back_stack = jnp.stack(
        [
            jnp.stack([back[:, :, 0], -back[:, :, 1]], axis=2),
            jnp.stack([back[:, :, 1], back[:, :, 0]], axis=2),
        ],
        axis=2,
    )
    numer = jnp.einsum("icopm,iprm->corm", back_stack, weighted, preferred_element_type=jnp.float32)
    numer = numer.reshape(class_count, 2 * cycle_total * harmonics)
    numer_share = lax.psum_scatter(numer, "dp", scatter_dimension=1, tiled=True)
    mass = jnp.sum(posterior, axis=2)
    denom, masses = lax.psum(
        (jnp.dot(mass.T, power_weight, precision=hp), jnp.sum(mass, axis=0)), "dp"
    )
    width = numer_share.shape[1]
    denom_full = jnp.broadcast_to(
        denom[:, None, :, None], (class_count, 2, cycle_total, harmonics)
    ).reshape(class_count, 2 * cycle_total * harmonics)
    denom_share = lax.dynamic_slice_in_dim(denom_full, lax.axis_index("dp") * width, width, 1)
    new_references = numer_share / (denom_share + 1.0)
    occupancy = masses * (class_count * lax.axis_size("cls") / (img_count * lax.axis_size("dp")))
    return (new_references, occupancy, evidence)


def solution(mesh):
    placed = (P("dp", None, None, None), P("cls", None, None, None), P(), P("dp"), P(), P("cls"))
    return jax.shard_map(
        shards,
        mesh=mesh,
        in_specs=placed,
        out_specs=(P("cls", "dp"), P("cls"), P("dp")),
        check_vma=False,
    )
```

profile of v0, /device:TPU:24, one launch (start us, length us, event | category | flops | bytes accessed | tf_op | source)
XLA Modules:
  0.0 291.6 jit_solution(15754659494439648385)
XLA Ops:
  7.3 1.4 multiply_reduce_fusion
  8.7 1.9 fusion.27
  10.6 3.0 %copy.40 = bf16[16,2,48,256]{2,0,1,3:T(8,128)(2,1)S(1)} copy(bf16[16,2,48,256]{3,2,1,0:T(8,128)(2,1)S(1)} %copy-done.1) | data formatting | bytes 1572864 | tf_op args[1]
  14.2 3.9 %fusion.4 = bf16[80,2,48,256,1]{3,2,1,0,4:T(8,128)(2,1)} fusion(bf16[80,2,48,256]{3,2,1,0:T(8,128)(2,1)} %param.6, f32[80,48]{1,0:T(8,128)S(1)} %copy.39), kind=kLoop, calls=%fused_computation.5 | loop fusion | flops 5898240 | bytes 7879680 | tf_op jit(solution)/shard_map/convert_element_type | solution.py:35
  18.1 8.9 %copy.52 = bf16[80,2,48,256,1]{0,2,1,4,3:T(8,128)(2,1)} copy(bf16[80,2,48,256,1]{3,2,1,0,4:T(8,128)(2,1)} %fusion.4) | data formatting | bytes 7864320 | tf_op jit(solution)/shard_map/convert_element_type | solution.py:35
  27.3 1.1 pad_maximum_fusion.1
  28.4 3.8 %copy.41 = bf16[16,2,48,256]{2,0,1,3:T(8,128)(2,1)} copy(bf16[16,2,48,256]{3,2,1,0:T(8,128)(2,1)S(1)} %pad_maximum_fusion.1) | data formatting | bytes 1572864 | tf_op jit(solution)/shard_map/stack | solution.py:36
  32.2 7.3 %fusion.5 = f32[80,16,2,256]{0,1,2,3:T(8,128)} fusion(bf16[80,2,48,256,1]{0,2,1,4,3:T(8,128)(2,1)} %copy.52, bf16[16,1,2,48,256]{3,0,2,1,4:T(8,128)(2,1)} %bitcast.48, bf16[16,1,2,48,256]{3,0,2,1,4:T(8,128)(2,1)S(1)} %bitcast.47), kind=kOutput, calls=%fused_computation.7 | convolution fusion | flops 126615552 | bytes 8126464 | tf_op jit(solution)/shard_map/iprm,cqprm->icqm/dot_general | solution.py:38
  39.5 5.3 %copy.43 = f32[80,16,2,256]{3,2,1,0:T(2,128)} copy(f32[80,16,2,256]{0,1,2,3:T(8,128)} %fusion.5) | data formatting | bytes 5242880 | tf_op jit(solution)/shard_map/iprm,cqprm->icqm/transpose | solution.py:38
  44.8 3.6 %dot_general.27 = f32[80,16,512]{2,1,0:T(8,128)S(1)} reshape(f32[80,16,2,256]{3,2,1,0:T(2,128)} %copy.43) | data formatting | bytes 5242880 | tf_op jit(solution)/shard_map/dot_general | solution.py:39
  48.4 2.6 fusion.28
  51.0 29.5 %pmax.7 = f32[80]{0:T(128)S(1)} all-reduce(f32[80]{0:T(128)S(1)} %get-tuple-element.16), channel_id=1, replica_groups=mesh['dp'=32,'cls'=16] {'cls'}, use_global_device_ids=true, to_apply=%region_2.3 | all-reduce | flops 80 | bytes 640 | tf_op jit(solution)/shard_map/pmax | solution.py:47
  80.5 1.2 exponential_reduce_fusion
  81.7 35.7 %psum.21 = f32[80]{0:T(128)S(1)} all-reduce(f32[80]{0:T(128)S(1)} %exponential_reduce_fusion), channel_id=1, replica_groups=mesh['dp'=32,'cls'=16] {'cls'}, use_global_device_ids=true, to_apply=%region_4.5 | all-reduce | flops 80 | bytes 640 | tf_op jit(solution)/shard_map/psum | solution.py:48
  117.5 2.3 convolution_convert_fusion
  120.3 6.3 %copy.47 = bf16[80,16,2,2,256]{0,1,3,2,4:T(8,128)(2,1)} copy(bf16[80,16,2,2,256]{4,1,3,0,2:T(8,128)(2,1)S(1)} %pad_maximum_fusion) | data formatting | bytes 5242880 | tf_op jit(solution)/shard_map/stack | solution.py:55
  126.6 7.9 %convolution_bitcast_fusion = f32[16,2,48,256]{2,0,1,3:T(8,128)} fusion(bf16[80,2,48,256,1]{0,2,1,4,3:T(8,128)(2,1)} %copy.52, bf16[80,16,2,2,256]{0,1,3,2,4:T(8,128)(2,1)} %copy.47), kind=kOutput, calls=%fused_computation.8 | convolution fusion | flops 125829120 | bytes 8126464 | tf_op jit(solution)/shard_map/icopm,iprm->corm/dot_general | solution.py:62
  134.5 3.5 %copy.48 = f32[16,2,48,256]{3,2,1,0:T(8,128)S(1)} copy(f32[16,2,48,256]{2,0,1,3:T(8,128)} %convolution_bitcast_fusion) | data formatting | bytes 3145728 | tf_op jit(solution)/shard_map/icopm,iprm->corm/transpose | solution.py:62
  138.0 2.1 copy.58
  140.8 72.4 %all-reduce = (f32[16,48]{1,0:T(8,128)S(1)}, f32[16]{0:T(128)S(1)}) all-reduce(f32[16,48]{1,0:T(8,128)S(1)} %fusion.25, f32[16]{0:T(128)S(1)} %get-tuple-element.3), channel_id=1, replica_groups=mesh['dp'=32,'cls'=16] {'dp'}, use_global_device_ids=true, to_apply=%region_7.8 | all-reduce | flops 784 | bytes 6272 | tf_op jit(solution)/shard_map/psum | solution.py:66
  213.4 0.9 copy.59
  214.3 0.5 broadcast_multiply_fusion
  214.8 68.5 %reduce-scatter.2.cloned.1.call-done = f32[16,768]{1,0:T(8,128)} async-done(((f32[16,24576]{1,0:T(8,128)}), f32[16,768]{1,0:T(8,128)}) %reduce-scatter.2.cloned.1.call-update) | async-done | bytes 49168 | tf_op jit(solution)/shard_map/reduce_scatter | solution.py:64
  283.4 1.4 add_divide_fusion
  (29 shorter events, 2.4 us)
Async XLA Ops:
  7.2 6.7 %copy-start = (f32[64,48]{0,1:T(8,128)S(1)}, f32[64,48]{0,1:T(8,128)}, u32[]{:S(2)}) copy-start(f32[64,48]{0,1:T(8,128)} %param.8) | copy-start | bytes 36868
  7.2 3.4 %copy-start.1 = (bf16[16,2,48,256]{3,2,1,0:T(8,128)(2,1)S(1)}, bf16[16,2,48,256]{3,2,1,0:T(8,128)(2,1)}, u32[]{:S(2)}) copy-start(bf16[16,2,48,256]{3,2,1,0:T(8,128)(2,1)} %param.7) | copy-start | bytes 2359300
  7.2 6.6 %copy-start.5 = (f32[48]{0:T(128)S(1)}, f32[48]{0:T(128)}, u32[]{:S(2)}) copy-start(f32[48]{0:T(128)} %param.10) | copy-start | bytes 580
  7.2 6.6 %copy-start.3 = (s32[80]{0:T(128)S(1)}, s32[80]{0:T(128)}, u32[]{:S(2)}) copy-start(s32[80]{0:T(128)} %param.9) | copy-start | bytes 964
  7.2 276.1 %reduce-scatter.2.cloned.1.call-start = ((), (), s32[]{:S(2)}) async-start(), calls=%async_computation.1 | async-start | bytes 1622016 | tf_op jit(solution)/shard_map/reduce_scatter | solution.py:64
  18.1 8.9 %copy-start.4 = (f32[16]{0:T(128)S(1)}, f32[16]{0:T(128)}, u32[]{:S(2)}) copy-start(f32[16]{0:T(128)} %param.11) | copy-start | bytes 196
  117.4 22.7 %copy-start.2 = (f32[80]{0:T(128)}, f32[80]{0:T(128)S(1)}, u32[]{:S(2)}) copy-start(f32[80]{0:T(128)S(1)} %log_add_fusion) | copy-start | bytes 964
Sparse Core Ops, SparseCore 0:
  140.2 143.1 reduce-scatter.1
where the time goes:
time: 292 us
  blocking collectives  138 us (47%)
  waiting for transfers between devices  68.5 us (23%)
  local copies, waits for them, and re-layouts  37.8 us (13%)
  matrix products  20.7 us (7%)
  between operations  14.2 us (5%)
  other arithmetic  12.7 us (4%)
    psum x1, blocking collectives, shards(): lax.psum((jnp.dot(mass.T, power_weight, precision=hp), jnp.sum(mass, axis...  72.4 us
    reduce_scatter x1, waiting for transfers between devices, shards(): numer_share = lax.psum_scatter(numer, 'dp', scatter_dimension=1, tiled=True)  68.5 us
    psum x1, blocking collectives, shards(): lax.psum(jnp.sum(jnp.exp(score - peak[:, None, None]), axis=(1, 2)), 'cls')  35.7 us
    pmax x1, blocking collectives, shards(): peak = lax.pmax(local_peak, 'cls')  29.5 us
    convert_element_type x1, local copies, waits for them, and re-layouts, shards(): (images.astype(jnp.float32) * weight[:, None, :, None]).astype(jnp.bfloat16)  8.89 us
    dot_general x1, matrix products, shards(): jnp.einsum('icopm,iprm->corm', back_stack, weighted, preferred_element_ty...  7.86 us
    dot_general x1, matrix products, shards(): jnp.einsum('iprm,cqprm->icqm', weighted, stacked, preferred_element_type=...  7.31 us
    another operation x1, local copies, waits for them, and re-layouts, shards(): jnp.stack([jnp.stack([back[:, :, 0], -back[:, :, 1]], axis=2), jnp.stack(...  6.33 us
  transfers between devices with their start and end apart: 1, of which 1 were waited for; matrix products, arithmetic and copies ran while one was open for 1% of the time, Pallas kernels for 0%

commit v1 on v0

v1 whole, which is shorter than its diff:
```python
import functools
import math

import jax
import jax.numpy as jnp
from jax import lax
from jax.experimental import pallas as pl
from jax.experimental.pallas import tpu as pltpu
from jax.sharding import PartitionSpec as P

ROT = 36
HALF = ROT // 2
LANES = 128
SIDE = 64
HP = lax.Precision.HIGHEST
F32 = jnp.float32
BF16 = jnp.bfloat16
NT = (((1,), (1,)), ((), ()))
TN = (((0,), (0,)), ((), ()))
MESH = pl.DeviceIdType.MESH


def iota(shape, dim):
    return lax.broadcasted_iota(jnp.int32, shape, dim)


def half_transform(even, odd):
    quarter = HALF // 2
    even_sum = [even[b] + even[HALF - b] for b in range(quarter)]
    even_diff = [even[b] - even[HALF - b] for b in range(quarter)]
    odd_sum = [None] + [odd[b] + odd[HALF - b] for b in range(1, quarter)]
    odd_diff = [None] + [odd[b] - odd[HALF - b] for b in range(1, quarter)]
    cosines, sines = [], []
    for k in range(HALF + 1):
        source = even_sum if k % 2 == 0 else even_diff
        total = source[0]
        for b in range(1, quarter):
            total = total + source[b] * math.cos(math.pi * ((b * k) % ROT) / HALF)
        if k % 2 == 0:
            total = total + even[quarter] * (1.0 if k % 4 == 0 else -1.0)
        cosines.append(total)
    for k in range(HALF + 1):
        if k in (0, HALF):
            sines.append(None)
            continue
        source = odd_sum if k % 2 == 1 else odd_diff
        total = source[1] * math.sin(math.pi * k / HALF)
        for b in range(2, quarter):
            total = total + source[b] * math.sin(math.pi * ((b * k) % ROT) / HALF)
        if k % 2 == 1:
            total = total + odd[quarter] * (1.0 if k % 4 == 1 else -1.0)
        sines.append(total)
    return cosines, sines


def folds(harmonics):
    return -(-harmonics // ROT)


def score_kernel(
    image_ref, refs_ref, ids_ref, ctf_ref, noise_ref, prior_ref,
    w_ref, score_ref, stats_ref, power_ref,
    x_ref, xr_ref, s_ref,
):
    images, _, cycles, harm = image_ref.shape
    classes = refs_ref.shape[0]
    groups = ctf_ref.shape[0]
    count = folds(harm)
    rows = count * ROT
    onehot = (iota((groups, images), 0) == ids_ref[...]).astype(F32)
    ctf = lax.dot_general(onehot, ctf_ref[...], TN, precision=HP, preferred_element_type=F32)
    power = ctf * ctf / noise_ref[...]
    spread = (iota((cycles, LANES), 1) % SIDE == iota((cycles, LANES), 0)).astype(F32)
    weight = jnp.dot(ctf / noise_ref[...], spread, precision=HP, preferred_element_type=F32)
    power_lanes = jnp.dot(power, spread, precision=HP, preferred_element_type=F32)
    share = power_ref.shape[0] // 8
    share = cycles // share
    row = iota((power_ref.shape[0], cycles), 0)
    pick = ((row // 8) * share + row % 8 == iota((power_ref.shape[0], cycles), 1)) & (row % 8 < share)
    by_dest = lax.dot_general(pick.astype(F32), power, NT, precision=HP, preferred_element_type=F32)
    power_ref[...] = by_dest + (iota(by_dest.shape, 0) % 8 == share).astype(F32)

    eye = (iota((harm, harm), 0) == iota((harm, harm), 1)).astype(BF16)
    gap = jnp.zeros((SIDE - cycles, harm), BF16)

    def move(first, second, out_ref, at0, at1):
        block = jnp.concatenate([first[0], gap, first[1], gap, second[0], gap, second[1], gap], axis=0)
        turned = lax.dot_general(eye, block, NT, preferred_element_type=F32)
        out_ref[pl.ds(at0 * rows, harm), :] = turned[:, :LANES]
        out_ref[pl.ds(at1 * rows, harm), :] = turned[:, LANES:]
        if rows > harm:
            out_ref[pl.ds(at0 * rows + harm, rows - harm), :] = jnp.zeros((rows - harm, LANES), F32)
            out_ref[pl.ds(at1 * rows + harm, rows - harm), :] = jnp.zeros((rows - harm, LANES), F32)

    @pl.loop(0, images // 2)
    def _(pair):
        i = pair * 2
        move(
            (image_ref[i, 0], image_ref[i, 1]), (image_ref[i + 1, 0], image_ref[i + 1, 1]), x_ref, i, i + 1
        )

    @pl.loop(0, classes)
    def _(c):
        real, imag = refs_ref[c, 0], refs_ref[c, 1]
        move((real, imag), (imag, -real), xr_ref, c, classes + c)

    def one_residue(b, squares):
        image_parts, ref_parts = [], []
        for a in range(count):
            at = b + ROT * a
            x = x_ref[pl.ds(at, images, stride=rows), :] * weight
            r = xr_ref[pl.ds(at, 2 * classes, stride=rows), :]
            squares = squares + r[:classes] * r[:classes]
            x, r = x.astype(BF16), r.astype(BF16)
            w_ref[b, :, a * LANES : (a + 1) * LANES] = x
            image_parts.append(x)
            ref_parts.append(r)
        s_ref[b] = lax.dot_general(
            jnp.concatenate(ref_parts, axis=1),
            jnp.concatenate(image_parts, axis=1),
            NT,
            preferred_element_type=F32,
        )
        return squares

    squares = lax.fori_loop(0, ROT, one_residue, jnp.zeros((classes, LANES), F32))
    model = lax.dot_general(squares, power_lanes, NT, precision=HP, preferred_element_type=F32)
    log_prior = jnp.sum(
        jnp.where(iota((classes, classes), 0) == iota((classes, classes), 1), jnp.log(prior_ref[...]), 0.0),
        axis=1,
        keepdims=True,
    )
    base = log_prior - 0.5 * model
    real = [s_ref[b, :classes] for b in range(ROT)]
    imag = [s_ref[b, classes:] for b in range(ROT)]
    even = [real[0]] + [real[b] + real[ROT - b] for b in range(1, HALF)] + [real[HALF]]
    odd = [None] + [imag[b] - imag[ROT - b] for b in range(1, HALF)]
    cosines, sines = half_transform(even, odd)
    peak = None
    for k in range(HALF + 1):
        if sines[k] is None:
            made = [(k, cosines[k] + base)]
        else:
            centre = cosines[k] + base
            made = [(k, centre + sines[k]), (ROT - k, centre - sines[k])]
        for at, value in made:
            score_ref[at] = value
            peak = value if peak is None else jnp.maximum(peak, value)
    peak = jnp.max(peak, axis=0, keepdims=True)
    total = jnp.zeros((classes, images), F32)
    for k in range(ROT):
        total = total + jnp.exp(score_ref[k] - peak)
    total = jnp.sum(total, axis=0, keepdims=True)
    stats_ref[...] = jnp.zeros(stats_ref.shape, F32)
    stats_ref[0:1, 0:images] = peak
    stats_ref[1:2, 0:images] = total


def update_kernel(
    scale, w_ref, score_ref, stats_ref, power_ref,
    out_ref, occ_ref, evidence_ref,
    gath_ref, back_ref, y_ref, t_ref, l_ref, r_ref, last_ref,
    gath_send, gath_recv, ring_send, ring_recv, last_send, last_recv,
):
    classes, images = score_ref.shape[1:]
    halves = t_ref.shape[0]
    harm = halves * LANES
    count = w_ref.shape[2] // LANES
    rows = count * ROT
    depth = l_ref.shape[0]
    share = out_ref.shape[1] // harm
    blocks = out_ref.shape[1] // LANES
    dp, cls = lax.axis_index("dp"), lax.axis_index("cls")
    n_cls = lax.axis_size("cls")
    x, z = dp // depth, dp % depth

    def at_z(step):
        return (z + step + depth) % depth

    up, down = x * depth + at_z(1), x * depth + at_z(-1)
    across = (1 - x) * depth + z
    barrier = pltpu.get_barrier_semaphore()
    for j in range(1, n_cls):
        pl.semaphore_signal(barrier, inc=1, device_id={"dp": dp, "cls": (cls + j) % n_cls}, device_id_type=MESH)
    for other in (up, down, across):
        pl.semaphore_signal(barrier, inc=1, device_id={"dp": other, "cls": cls}, device_id_type=MESH)
    pl.semaphore_wait(barrier, n_cls - 1 + 3)

    sends = []
    for j in range(1, n_cls):
        copy = pltpu.make_async_remote_copy(
            src_ref=stats_ref,
            dst_ref=gath_ref.at[j],
            send_sem=gath_send.at[j],
            recv_sem=gath_recv.at[j],
            device_id={"dp": dp, "cls": (cls + j) % n_cls},
            device_id_type=MESH,
        )
        copy.start()
        sends.append(copy)
    for copy in sends:
        copy.wait_recv()
    parts = [stats_ref[...]] + [gath_ref[j] for j in range(1, n_cls)]
    peak = parts[0][0:1, :images]
    for part in parts[1:]:
        peak = jnp.maximum(peak, part[0:1, :images])
    total = jnp.zeros((1, images), F32)
    for part in parts:
        total = total + part[1:2, :images] * jnp.exp(part[0:1, :images] - peak)
    evidence = peak + jnp.log(total)
    evidence_ref[...] = evidence

    posterior = [jnp.exp(score_ref[k] - evidence) for k in range(ROT)]
    even = [posterior[0]] + [posterior[k] + posterior[ROT - k] for k in range(1, HALF)] + [posterior[HALF]]
    odd = [None] + [posterior[k] - posterior[ROT - k] for k in range(1, HALF)]
    cosines, sines = half_transform(even, odd)
    mass = cosines[0]
    for b in range(HALF + 1):
        real = cosines[b].astype(BF16)
        imag = jnp.zeros((classes, images), BF16) if sines[b] is None else sines[b].astype(BF16)
        back_ref[b] = jnp.concatenate([real, imag], axis=0)
        if 0 < b < HALF:
            back_ref[ROT - b] = jnp.concatenate([real, -imag], axis=0)
    denominators = lax.dot_general(power_ref[...], mass, NT, precision=HP, preferred_element_type=F32)

    sign = jnp.where(iota((classes, LANES), 1) < SIDE, -1.0, 1.0)

    @pl.loop(0, ROT)
    def _(b):
        both = jnp.dot(back_ref[b], w_ref[b], preferred_element_type=F32)
        for a in range(count):
            piece = both[:, a * LANES : (a + 1) * LANES]
            y_ref[pl.ds(b + ROT * a, classes, stride=rows), :] = piece[:classes] + sign * pltpu.roll(
                piece[classes:], SIDE, 1
            )

    @pl.loop(0, classes)
    def _(c):
        for h in range(halves):
            t_ref[h, pl.ds(pl.multiple_of(c * LANES, LANES), LANES), :] = y_ref[
                pl.ds(pl.multiple_of(c * rows + h * LANES, 8), LANES), :
            ].T

    for dest in range(depth):
        for p in range(2):
            for j in range(share):
                row = p * SIDE + dest * share + j
                for h in range(halves):
                    l_ref[dest, p, (j * halves + h) * classes : (j * halves + h + 1) * classes, :] = t_ref[
                        h, pl.ds(row, classes, stride=LANES), :
                    ]
            tail = l_ref.shape[2] - 8
            l_ref[dest, p, tail:, :] = jnp.zeros((8, LANES), F32)
            l_ref[dest, p, tail:, 0:classes] = denominators[dest * 8 : dest * 8 + 8]

    hops = depth // 2
    streams = [(1, 0, hops), (-1, 1, hops), (1, 1, hops - 1), (-1, 0, hops - 1)]

    def hop(index, t, source):
        step, p, _ = streams[index]
        return pltpu.make_async_remote_copy(
            src_ref=source,
            dst_ref=r_ref.at[index, t],
            send_sem=ring_send.at[index, t],
            recv_sem=ring_recv.at[index, t],
            device_id={"dp": up if step == 1 else down, "cls": cls},
            device_id_type=MESH,
        )

    for index, (step, p, length) in enumerate(streams):
        hop(index, 0, l_ref.at[at_z(step * length), p]).start()

    def one_hop(t, carry):
        for index, (step, p, length) in enumerate(streams):

            def go():
                hop(index, t - 1, l_ref.at[0, p]).wait_recv()
                r_ref[index, t - 1] = r_ref[index, t - 1] + l_ref[at_z(step * (length - t)), p]
                hop(index, t, r_ref.at[index, t - 1]).start()

            if length == hops:
                go()
            else:
                pl.when(t < length)(go)
        return carry

    lax.fori_loop(1, hops, one_hop, 0)
    for index, (step, p, length) in enumerate(streams):
        hop(index, length - 1, l_ref.at[0, p]).wait_recv()
    ends = [streams[index][2] - 1 for index in range(4)]
    sums = [
        l_ref[z, 0] + r_ref[0, ends[0]] + r_ref[3, ends[3]],
        l_ref[z, 1] + r_ref[1, ends[1]] + r_ref[2, ends[2]],
    ]
    last_ref[0] = jnp.where(x == 0, sums[1], sums[0])
    copy = pltpu.make_async_remote_copy(
        src_ref=last_ref.at[0],
        dst_ref=last_ref.at[1],
        send_sem=last_send,
        recv_sem=last_recv,
        device_id={"dp": across, "cls": cls},
        device_id_type=MESH,
    )
    copy.start()
    mine = jnp.where(x == 0, sums[0], sums[1])
    copy.wait_recv()
    mine = mine + last_ref[1]
    tail = mine[blocks * classes :, :]
    occ_ref[...] = tail[share : share + 1, 0:classes] * scale
    columns = jnp.concatenate([tail, jnp.zeros((LANES - 8, LANES), F32)], axis=0).T
    for j in range(share):
        below = columns[:classes, j : j + 1] + 1.0
        for h in range(halves):
            q = j * halves + h
            out_ref[:, q * LANES : (q + 1) * LANES] = mine[q * classes : (q + 1) * classes] / below
    copy.wait_send()
    for send in sends:
        send.wait_send()
    for index, (step, p, length) in enumerate(streams):

        def drained(t, carry):
            hop(index, t, l_ref.at[0, p]).wait_send()
            return carry

        lax.fori_loop(0, length, drained, 0)


def vmem(count):
    return [pl.BlockSpec(memory_space=pltpu.VMEM)] * count


def shards(images, references, ctf_rows, group_ids, noise_var, class_prior):
    img_count, _, cycles, harm = images.shape
    classes = references.shape[0]
    n_dp, n_cls = lax.axis_size("dp"), lax.axis_size("cls")
    depth = n_dp // 2
    share = cycles // depth
    count = folds(harm)
    rows = count * ROT
    width = share * harm
    w, score, stats, power = pl.pallas_call(
        score_kernel,
        out_shape=[
            jax.ShapeDtypeStruct((ROT, img_count, count * LANES), BF16),
            jax.ShapeDtypeStruct((ROT, classes, img_count), F32),
            jax.ShapeDtypeStruct((8, LANES), F32),
            jax.ShapeDtypeStruct((depth * 8, img_count), F32),
        ],
        in_specs=vmem(6),
        out_specs=vmem(4),
        scratch_shapes=[
            pltpu.VMEM((img_count * rows, LANES), F32),
            pltpu.VMEM((2 * classes * rows, LANES), F32),
            pltpu.VMEM((ROT, 2 * classes, img_count), F32),
        ],
        compiler_params=pltpu.CompilerParams(vmem_limit_bytes=48 * 2**20),
    )(
        images, references, group_ids.reshape(1, -1), ctf_rows, noise_var.reshape(1, -1),
        class_prior.reshape(1, -1),
    )
    chunk = width // LANES * classes + 8
    new_references, occupancy, evidence = pl.pallas_call(
        functools.partial(update_kernel, classes * n_cls / (img_count * n_dp)),
        out_shape=[
            jax.ShapeDtypeStruct((classes, width), F32),
            jax.ShapeDtypeStruct((1, classes), F32),
            jax.ShapeDtypeStruct((1, img_count), F32),
        ],
        in_specs=vmem(4),
        out_specs=vmem(3),
        scratch_shapes=[
            pltpu.VMEM((n_cls, 8, LANES), F32),
            pltpu.VMEM((ROT, 2 * classes, img_count), BF16),
            pltpu.VMEM((classes * rows, LANES), F32),
            pltpu.VMEM((harm // LANES, classes * LANES, LANES), F32),
            pltpu.VMEM((depth, 2, chunk, LANES), F32),
            pltpu.VMEM((4, depth // 2, chunk, LANES), F32),
            pltpu.VMEM((2, chunk, LANES), F32),
            pltpu.SemaphoreType.DMA((n_cls,)),
            pltpu.SemaphoreType.DMA((n_cls,)),
            pltpu.SemaphoreType.DMA((4, depth // 2)),
            pltpu.SemaphoreType.DMA((4, depth // 2)),
            pltpu.SemaphoreType.DMA,
            pltpu.SemaphoreType.DMA,
        ],
        compiler_params=pltpu.CompilerParams(
            collective_id=0, has_side_effects=True, vmem_limit_bytes=48 * 2**20
        ),
    )(w, score, stats, power)
    return new_references, occupancy.reshape(-1), evidence.reshape(-1)


def solution(mesh):
    placed = (P("dp", None, None, None), P("cls", None, None, None), P(), P("dp"), P(), P("cls"))
    return jax.shard_map(
        shards,
        mesh=mesh,
        in_specs=placed,
        out_specs=(P("cls", "dp"), P("cls"), P("dp")),
        check_vma=False,
    )
```

time: 292 us -> 103 us (0.35)
  the two profiles are of different devices: /device:TPU:24 before, /device:TPU:4 now
where the time goes in v1:
time: 103 us
  Pallas kernels  94.6 us (92%)
  local copies, waits for them, and re-layouts  7.67 us (7%)
    pallas_call x1, Pallas kernels, shards(): pl.pallas_call(functools.partial(update_kernel, classes * n_cls / (img_co...  65.7 us
    pallas_call x1, Pallas kernels, shards(): pl.pallas_call(score_kernel, out_shape=[jax.ShapeDtypeStruct((ROT, img_co...  28.9 us
    unnamed x14, local copies, waits for them, and re-layouts  7.67 us

profile of v1, /device:TPU:4, one launch (start us, length us, event | category | flops | bytes accessed | tf_op | source)
XLA Modules:
  0.0 102.9 jit_solution(15804294192023404719)
XLA Ops:
  0.6 0.8 copy.9.ctf_ref
  1.4 0.0 copy-start
  1.5 2.1 %copy-done = bf16[80,2,48,256]{3,2,1,0:T(8,128)(2,1)S(1)} copy-done((bf16[80,2,48,256]{3,2,1,0:T(8,128)(2,1)S(1)}, bf16[80,2,48,256]{3,2,1,0:T(8,128)(2,1)}, u32[]{:S(2)}) %copy-start) | copy-done | bytes 3932184
  3.6 0.0 copy-start.1
  3.6 1.1 %copy-done.1 = bf16[16,2,48,256]{3,2,1,0:T(8,128)(2,1)S(1)} copy-done((bf16[16,2,48,256]{3,2,1,0:T(8,128)(2,1)S(1)}, bf16[16,2,48,256]{3,2,1,0:T(8,128)(2,1)}, u32[]{:S(2)}) %copy-start.1) | copy-done | bytes 786456
  4.7 0.0 copy-start.2
  4.7 0.7 copy-done.2
  5.4 0.0 copy-start.3
  5.4 0.7 copy-done.3
  6.0 0.0 copy-start.4
  6.0 0.7 copy-done.4
  6.7 28.9 %shard_map.85 = (bf16[36,80,1024]{2,1,0:T(8,128)(2,1)}, f32[36,16,80]{2,1,0:T(8,128)S(1)}, f32[8,128]{1,0:T(8,128)S(1)}, f32[128,80]{1,0:T(8,128)S(1)}) custom-call(bf16[80,2,48,256]{3,2,1,0:T(8,128)(2,1)S(1)} %copy-done, bf16[16,2,48,256]{3,2,1,0:T(8,128)(2,1)S(1)} %copy-done.1, s32[1,80]{1,0:T(1,128)S(1)} %bitcast.5, f32[64,48]{1,0:T(8,128)S(1)} %copy.9.ctf_ref, ...), custom_call_target="tpu_custom_call" | custom-call | tf_op jit(solution)/shard_map/pallas_call | solution.py:341
  35.5 65.7 %shard_map.86 = (f32[16,768]{1,0:T(8,128)S(1)}, f32[1,16]{1,0:T(1,128)S(1)}, f32[1,80]{1,0:T(1,128)S(1)}) custom-call(bf16[36,80,1024]{2,1,0:T(8,128)(2,1)} %get-tuple-element.10.w_ref, f32[36,16,80]{2,1,0:T(8,128)S(1)} %get-tuple-element.11.score_ref, f32[8,128]{1,0:T(8,128)S(1)} %get-tuple-element.12.stats_ref, f32[128,80]{1,0:T(8,128)S(1)} %get-tuple-element.13.power_ref), custom_call_target="tpu_custom_call" | custom-call | tf_op jit(solution)/shard_map/pallas_call | solution.py:362
  101.3 0.6 copy.13
  101.9 0.5 copy.14
  102.4 0.5 copy.15
Async XLA Ops:
  1.4 2.1 %copy-start = (bf16[80,2,48,256]{3,2,1,0:T(8,128)(2,1)S(1)}, bf16[80,2,48,256]{3,2,1,0:T(8,128)(2,1)}, u32[]{:S(2)}) copy-start(bf16[80,2,48,256]{3,2,1,0:T(8,128)(2,1)} %image_ref.1) | copy-start | bytes 11796484
  3.6 1.1 %copy-start.1 = (bf16[16,2,48,256]{3,2,1,0:T(8,128)(2,1)S(1)}, bf16[16,2,48,256]{3,2,1,0:T(8,128)(2,1)}, u32[]{:S(2)}) copy-start(bf16[16,2,48,256]{3,2,1,0:T(8,128)(2,1)} %refs_ref.1) | copy-start | bytes 2359300
  4.7 0.7 copy-start.2
  5.4 0.7 copy-start.3
  6.0 0.7 copy-start.4

commit v2 on v1

v2 whole, which is shorter than its diff:
```python
import functools
import math

import jax
import jax.numpy as jnp
from jax import lax
from jax.experimental import pallas as pl
from jax.experimental.pallas import tpu as pltpu
from jax.sharding import PartitionSpec as P

ROT = 36
HALF = ROT // 2
LANES = 128
SIDE = 64
HP = lax.Precision.HIGHEST
F32 = jnp.float32
BF16 = jnp.bfloat16
NT = (((1,), (1,)), ((), ()))
TN = (((0,), (0,)), ((), ()))
MESH = pl.DeviceIdType.MESH


def iota(shape, dim):
    return lax.broadcasted_iota(jnp.int32, shape, dim)


def half_transform(even, odd):
    quarter = HALF // 2
    even_sum = [even[b] + even[HALF - b] for b in range(quarter)]
    even_diff = [even[b] - even[HALF - b] for b in range(quarter)]
    odd_sum = [None] + [odd[b] + odd[HALF - b] for b in range(1, quarter)]
    odd_diff = [None] + [odd[b] - odd[HALF - b] for b in range(1, quarter)]
    cosines, sines = [], []
    for k in range(HALF + 1):
        source = even_sum if k % 2 == 0 else even_diff
        total = source[0]
        for b in range(1, quarter):
            total = total + source[b] * math.cos(math.pi * ((b * k) % ROT) / HALF)
        if k % 2 == 0:
            total = total + even[quarter] * (1.0 if k % 4 == 0 else -1.0)
        cosines.append(total)
    for k in range(HALF + 1):
        if k in (0, HALF):
            sines.append(None)
            continue
        source = odd_sum if k % 2 == 1 else odd_diff
        total = source[1] * math.sin(math.pi * k / HALF)
        for b in range(2, quarter):
            total = total + source[b] * math.sin(math.pi * ((b * k) % ROT) / HALF)
        if k % 2 == 1:
            total = total + odd[quarter] * (1.0 if k % 4 == 1 else -1.0)
        sines.append(total)
    return cosines, sines


def folds(harmonics):
    return -(-harmonics // ROT)


def column(row):
    square = (row.shape[1], row.shape[1])
    return jnp.sum(jnp.where(iota(square, 0) == iota(square, 1), row, 0.0), axis=1, keepdims=True)


def reduction_tree():
    parent = {}
    for sign in (1, -1):
        for ox in (0, 1):
            for leaf, relay in ((7, 6), (5, 6), (4, 3), (2, 3)):
                parent[(ox, leaf * sign)] = (ox, relay * sign)
        for relay in (6, 3, 1):
            parent[(1, relay * sign)] = (0, relay * sign)
            parent[(0, relay * sign)] = (0, 0)
    parent[(0, 8)] = (0, 6)
    parent[(1, 8)] = (1, -6)
    parent[(1, 0)] = (0, 0)
    return parent


ORDER = (8, 7, -7, 5, -5, 4, -4, 2, -2, 6, -6, 3, -3, 1, -1, 0)
PIECES = 5
STRIDE = 289


def kernel(
    scale, image_hbm, refs_hbm, ids_hbm, ctf_hbm, noise_hbm, prior_hbm,
    out_ref, occ_ref, evidence_ref,
    image_ref, refs_ref, ids_ref, ctf_ref, noise_ref, prior_ref,
    x_ref, xr_ref, w_ref, s_ref, score_ref, stats_ref, gath_ref, back_ref, y_ref, t_ref, den_ref, l_ref, r_ref,
    load_sem, gath_send, gath_recv, tree_send, tree_recv,
):
    images, _, cycles, harm = image_ref.shape
    classes = refs_ref.shape[0]
    groups = ctf_ref.shape[1]
    count = folds(harm)
    rows = count * ROT
    depth = l_ref.shape[0]
    share = cycles // depth
    halves = harm // LANES
    blocks = share * halves
    piece = images // PIECES

    dp, cls = lax.axis_index("dp"), lax.axis_index("cls")
    n_cls = lax.axis_size("cls")
    x, z = dp // depth, dp % depth

    def at_z(step):
        return (z + step + depth) % depth

    def at_x(step):
        return (x + step) % 2

    loads = [
        pltpu.make_async_copy(source, target, load_sem.at[n])
        for n, (source, target) in enumerate(
            [(ids_hbm, ids_ref), (ctf_hbm, ctf_ref), (noise_hbm, noise_ref), (prior_hbm, prior_ref), (refs_hbm, refs_ref)]
            + [(image_hbm.at[pl.ds(n * piece, piece)], image_ref.at[pl.ds(n * piece, piece)]) for n in range(PIECES)]
        )
    ]
    for load in loads:
        load.start()

    parent = reduction_tree()
    index = {node: n for n, node in enumerate(parent)}
    children = {node: [other for other in parent if parent[other] == node] for node in [*parent, (0, 0)]}
    moves = {((parent[node][0] - node[0]) % 2, (parent[node][1] - node[1]) % depth) for node in parent}
    peers = sorted(moves | {(ox, -oz % depth) for ox, oz in moves})
    barrier = pltpu.get_barrier_semaphore()
    for ox, oz in peers:
        pl.semaphore_signal(
            barrier, inc=1, device_id={"dp": at_x(ox) * depth + at_z(oz), "cls": cls}, device_id_type=MESH
        )
    for j in range(1, n_cls):
        pl.semaphore_signal(barrier, inc=1, device_id={"dp": dp, "cls": (cls + j) % n_cls}, device_id_type=MESH)

    def clear(ref, total, unroll):
        @pl.loop(0, total, unroll=unroll)
        def _(i):
            ref[pl.ds(i * STRIDE + harm, rows - harm), :] = jnp.zeros((rows - harm, LANES), F32)

    clear(x_ref, images, 8)
    clear(xr_ref, 2 * classes, 8)

    for load in loads[:4]:
        load.wait()
    onehot = (iota((groups, images), 0) == ids_ref[...]).astype(F32)
    ctf = jnp.dot(ctf_ref[...], onehot, precision=HP, preferred_element_type=F32)
    noise = column(noise_ref[...])
    power = ctf * ctf / noise
    spread = (iota((cycles, LANES), 1) % SIDE == iota((cycles, LANES), 0)).astype(F32)
    weight = lax.dot_general(ctf / noise, spread, TN, precision=HP, preferred_element_type=F32)
    power_lanes = lax.dot_general(power, spread, TN, precision=HP, preferred_element_type=F32)
    shape = (depth * 8, cycles)
    row = iota(shape, 0)
    pick = ((row // 8) * share + row % 8 == iota(shape, 1)) & (row % 8 < share)
    by_dest = jnp.dot(pick.astype(F32), power, precision=HP, preferred_element_type=F32)
    by_dest = by_dest + (iota(by_dest.shape, 0) % 8 == share).astype(F32)
    log_prior = column(jnp.log(prior_ref[...]))

    eye = (iota((harm, harm), 0) == iota((harm, harm), 1)).astype(BF16)
    gap = jnp.zeros((SIDE - cycles, harm), BF16)

    def turn(first, second, ref, at0, at1):
        block = jnp.concatenate([first[0], gap, first[1], gap, second[0], gap, second[1], gap], axis=0)
        turned = lax.dot_general(eye, block, NT, preferred_element_type=F32)
        ref[pl.ds(at0 * STRIDE, harm), :] = turned[:, :LANES]
        ref[pl.ds(at1 * STRIDE, harm), :] = turned[:, LANES:]

    loads[4].wait()

    @pl.loop(0, classes, unroll=8)
    def _(c):
        real, imag = refs_ref[c, 0], refs_ref[c, 1]
        turn((real, imag), (imag, -real), xr_ref, c, classes + c)

    for n in range(PIECES):
        loads[5 + n].wait()

        @pl.loop(0, piece // 2, unroll=8)
        def _(pair):
            i = n * piece + pair * 2
            turn((image_ref[i, 0], image_ref[i, 1]), (image_ref[i + 1, 0], image_ref[i + 1, 1]), x_ref, i, i + 1)

    def one_residue(b, squares):
        image_parts, ref_parts = [], []
        for a in range(count):
            at = b + ROT * a
            x_part = (x_ref[pl.ds(at, images, stride=STRIDE), :] * weight).astype(BF16)
            r_part = xr_ref[pl.ds(at, 2 * classes, stride=STRIDE), :]
            squares = squares + r_part[:classes] * r_part[:classes]
            w_ref[b, :, a * LANES : (a + 1) * LANES] = x_part
            image_parts.append(x_part)
            ref_parts.append(r_part.astype(BF16))
        s_ref[b] = lax.dot_general(
            jnp.concatenate(ref_parts, axis=1),
            jnp.concatenate(image_parts, axis=1),
            NT,
            preferred_element_type=F32,
        )
        return squares

    squares = lax.fori_loop(0, ROT, one_residue, jnp.zeros((classes, LANES), F32), unroll=12)
    model = lax.dot_general(squares, power_lanes, NT, precision=HP, preferred_element_type=F32)
    base = log_prior - 0.5 * model
    real = [s_ref[b, :classes] for b in range(ROT)]
    imag = [s_ref[b, classes:] for b in range(ROT)]
    even = [real[0]] + [real[b] + real[ROT - b] for b in range(1, HALF)] + [real[HALF]]
    odd = [None] + [imag[b] - imag[ROT - b] for b in range(1, HALF)]
    cosines, sines = half_transform(even, odd)
    peak = None
    for k in range(HALF + 1):
        centre = cosines[k] + base
        made = [(k, centre)] if sines[k] is None else [(k, centre + sines[k]), (ROT - k, centre - sines[k])]
        for at, value in made:
            score_ref[at] = value
            peak = value if peak is None else jnp.maximum(peak, value)
    peak = jnp.max(peak, axis=0, keepdims=True)
    total = jnp.zeros((classes, images), F32)
    for k in range(ROT):
        total = total + jnp.exp(score_ref[k] - peak)
    stats_ref[...] = jnp.zeros(stats_ref.shape, F32)
    stats_ref[0:1, 0:images] = peak
    stats_ref[1:2, 0:images] = jnp.sum(total, axis=0, keepdims=True)

    pl.semaphore_wait(barrier, len(peers) + n_cls - 1)
    sends = []
    for j in range(1, n_cls):
        copy = pltpu.make_async_remote_copy(
            src_ref=stats_ref,
            dst_ref=gath_ref.at[j],
            send_sem=gath_send.at[j],
            recv_sem=gath_recv.at[j],
            device_id={"dp": dp, "cls": (cls + j) % n_cls},
            device_id_type=MESH,
        )
        copy.start()
        sends.append(copy)
    for copy in sends:
        copy.wait_recv()
    parts = [stats_ref[...]] + [gath_ref[j] for j in range(1, n_cls)]
    peak = parts[0][0:1, :images]
    for part in parts[1:]:
        peak = jnp.maximum(peak, part[0:1, :images])
    total = jnp.zeros((1, images), F32)
    for part in parts:
        total = total + part[1:2, :images] * jnp.exp(part[0:1, :images] - peak)
    evidence = peak + jnp.log(total)
    evidence_ref[...] = evidence

    posterior = [jnp.exp(score_ref[k] - evidence) for k in range(ROT)]
    even = [posterior[0]] + [posterior[k] + posterior[ROT - k] for k in range(1, HALF)] + [posterior[HALF]]
    odd = [None] + [posterior[k] - posterior[ROT - k] for k in range(1, HALF)]
    cosines, sines = half_transform(even, odd)
    mass = cosines[0]
    for b in range(HALF + 1):
        real = cosines[b].astype(BF16)
        imag = jnp.zeros((classes, images), BF16) if sines[b] is None else sines[b].astype(BF16)
        back_ref[b] = jnp.concatenate([real, imag], axis=0)
        if 0 < b < HALF:
            back_ref[ROT - b] = jnp.concatenate([real, -imag], axis=0)
    den_ref[...] = jnp.zeros(den_ref.shape, F32)
    den_ref[:, 0:classes] = lax.dot_general(by_dest, mass, NT, precision=HP, preferred_element_type=F32)

    sign = jnp.where(iota((classes, LANES), 1) < SIDE, -1.0, 1.0)

    @pl.loop(0, ROT, unroll=12)
    def _(b):
        both = jnp.dot(back_ref[b], w_ref[b], preferred_element_type=F32)
        for a in range(count):
            part = both[:, a * LANES : (a + 1) * LANES]
            y_ref[pl.ds(b + ROT * a, classes, stride=STRIDE), :] = part[:classes] + sign * pltpu.roll(
                part[classes:], SIDE, 1
            )

    @pl.loop(0, classes, unroll=4)
    def _(c):
        for h in range(halves):
            t_ref[h, pl.ds(pl.multiple_of(c * LANES, LANES), LANES), :] = y_ref[
                pl.ds(c * STRIDE + h * LANES, LANES), :
            ].T

    def towards(node, source):
        ox, oz = parent[node][0] - node[0], parent[node][1] - node[1]
        return pltpu.make_async_remote_copy(
            src_ref=source,
            dst_ref=r_ref.at[index[node]],
            send_sem=tree_send.at[index[node]],
            recv_sem=tree_recv.at[index[node]],
            device_id={"dp": at_x(ox % 2) * depth + at_z(oz % depth), "cls": cls},
            device_id_type=MESH,
        )

    def send(node):
        towards(node, l_ref.at[at_z(-node[1]), at_x(node[0])]).start()

    def gathered(node):
        value = l_ref[at_z(-node[1]), at_x(node[0])]
        for child in children[node]:
            towards(child, l_ref.at[0, 0]).wait_recv()
            value = value + r_ref[index[child]]
        return value

    def pass_on(node):
        l_ref[at_z(-node[1]), at_x(node[0])] = gathered(node)
        send(node)

    for oz in ORDER:
        dest = at_z(-oz)
        for p in range(2):
            for j in range(share):
                first = p * SIDE + dest * share + j
                for h in range(halves):
                    q = j * halves + h
                    l_ref[dest, p, q * classes : (q + 1) * classes, :] = t_ref[
                        h, pl.ds(first, classes, stride=LANES), :
                    ]
            l_ref[dest, p, blocks * classes :, :] = den_ref[pl.ds(pl.multiple_of(dest * 8, 8), 8), :]
        for ox in (0, 1):
            if (ox, oz) in parent and not children[(ox, oz)]:
                send((ox, oz))
    for node in ((1, 6), (1, -6), (1, 3), (1, -3), (0, 6), (0, -6), (0, 3), (0, -3), (0, 1), (0, -1)):
        pass_on(node)
    mine = gathered((0, 0))
    tail = mine[blocks * classes :, :]
    occ_ref[...] = tail[share : share + 1, 0:classes] * scale
    columns = jnp.concatenate([tail, jnp.zeros((LANES - 8, LANES), F32)], axis=0).T
    for j in range(share):
        below = columns[:classes, j : j + 1] + 1.0
        for h in range(halves):
            q = j * halves + h
            out_ref[:, q * LANES : (q + 1) * LANES] = mine[q * classes : (q + 1) * classes] / below
    for copy in sends:
        copy.wait_send()
    for node in parent:
        towards(node, l_ref.at[0, 0]).wait_send()


def shards(images, references, ctf_rows, group_ids, noise_var, class_prior):
    img_count, _, cycles, harm = images.shape
    classes = references.shape[0]
    n_dp, n_cls = lax.axis_size("dp"), lax.axis_size("cls")
    depth = n_dp // 2
    count = folds(harm)
    rows = count * ROT
    width = cycles // depth * harm
    chunk = width // LANES * classes + 8
    nodes = len(reduction_tree())
    args = (
        images, references, group_ids.reshape(1, -1), ctf_rows.T, noise_var.reshape(1, -1), class_prior.reshape(1, -1)
    )
    new_references, occupancy, evidence = pl.pallas_call(
        functools.partial(kernel, classes * n_cls / (img_count * n_dp)),
        out_shape=[
            jax.ShapeDtypeStruct((classes, width), F32),
            jax.ShapeDtypeStruct((1, classes), F32),
            jax.ShapeDtypeStruct((1, img_count), F32),
        ],
        in_specs=[pl.BlockSpec(memory_space=pl.ANY)] * len(args),
        out_specs=[pl.BlockSpec(memory_space=pltpu.VMEM)] * 3,
        scratch_shapes=[
            *[pltpu.VMEM(arg.shape, arg.dtype) for arg in args],
            pltpu.VMEM((img_count * STRIDE, LANES), F32),
            pltpu.VMEM((2 * classes * STRIDE, LANES), F32),
            pltpu.VMEM((ROT, img_count, count * LANES), BF16),
            pltpu.VMEM((ROT, 2 * classes, img_count), F32),
            pltpu.VMEM((ROT, classes, img_count), F32),
            pltpu.VMEM((8, LANES), F32),
            pltpu.VMEM((n_cls, 8, LANES), F32),
            pltpu.VMEM((ROT, 2 * classes, img_count), BF16),
            pltpu.VMEM((classes * STRIDE, LANES), F32),
            pltpu.VMEM((harm // LANES, classes * LANES, LANES), F32),
            pltpu.VMEM((depth * 8, LANES), F32),
            pltpu.VMEM((depth, 2, chunk, LANES), F32),
            pltpu.VMEM((nodes, chunk, LANES), F32),
            pltpu.SemaphoreType.DMA((5 + PIECES,)),
            pltpu.SemaphoreType.DMA((n_cls,)),
            pltpu.SemaphoreType.DMA((n_cls,)),
            pltpu.SemaphoreType.DMA((nodes,)),
            pltpu.SemaphoreType.DMA((nodes,)),
        ],
        compiler_params=pltpu.CompilerParams(
            collective_id=0, has_side_effects=True, vmem_limit_bytes=56 * 2**20
        ),
    )(*args)
    return new_references, occupancy.reshape(-1), evidence.reshape(-1)


def solution(mesh):
    placed = (P("dp", None, None, None), P("cls", None, None, None), P(), P("dp"), P(), P("cls"))
    return jax.shard_map(
        shards,
        mesh=mesh,
        in_specs=placed,
        out_specs=(P("cls", "dp"), P("cls"), P("dp")),
        check_vma=False,
    )
```

time: 103 us -> 60.5 us (0.59)
  the two profiles are of different devices: /device:TPU:4 before, /device:TPU:1 now
where the time goes in v2:
time: 60.5 us; the launch traced here: 60.3 us
  Pallas kernels  55.9 us (92%)
  local copies, waits for them, and re-layouts  3.68 us (6%)
  between operations  0.64 us (1%)
    pallas_call x1, Pallas kernels, shards(): pl.pallas_call(functools.partial(kernel, classes * n_cls / (img_count * n...  55.9 us
    unnamed x3, local copies, waits for them, and re-layouts  3.68 us

profile of v2, /device:TPU:1, one launch (start us, length us, event | category | flops | bytes accessed | tf_op | source)
XLA Modules:
  0.0 60.3 jit_solution(13038343535880115187)
XLA Ops:
  0.6 55.9 %shard_map.85 = (f32[16,768]{1,0:T(8,128)}, f32[1,16]{1,0:T(1,128)}, f32[1,80]{1,0:T(1,128)}) custom-call(bf16[80,2,48,256]{3,2,1,0:T(8,128)(2,1)} %image_hbm.1, bf16[16,2,48,256]{3,2,1,0:T(8,128)(2,1)} %refs_hbm.1, s32[1,80]{1,0:T(1,128)} %bitcast.7, f32[48,64]{1,0:T(8,128)} %bitcast.6, f32[1,48]{1,0:T(1,128)} %bitcast.8, f32[1,16]{1,0:T(1,128)} %bitcast.9), custom_call_target="tpu_custom_call" | custom-call | tf_op jit(solution)/shard_map/pallas_call | solution.py:351
  56.6 1.4 %copy.12 = f32[16,768]{1,0:T(8,128)} copy(f32[16,768]{1,0:T(8,128)} %get-tuple-element.12) | data formatting | bytes 98304
  58.0 1.1 %copy.13 = f32[16]{0:T(128)} copy(f32[16]{0:T(128)} %bitcast.11) | data formatting | bytes 128
  59.1 1.1 %copy.14 = f32[80]{0:T(128)} copy(f32[80]{0:T(128)} %bitcast.10) | data formatting | bytes 640

commit v3 on v2

--- a/solution.py
+++ b/solution.py
@@ -62,36 +62,27 @@
     return jnp.sum(jnp.where(iota(square, 0) == iota(square, 1), row, 0.0), axis=1, keepdims=True)
 
 
-def reduction_tree():
-    parent = {}
-    for sign in (1, -1):
-        for ox in (0, 1):
-            for leaf, relay in ((7, 6), (5, 6), (4, 3), (2, 3)):
-                parent[(ox, leaf * sign)] = (ox, relay * sign)
-        for relay in (6, 3, 1):
-            parent[(1, relay * sign)] = (0, relay * sign)
-            parent[(0, relay * sign)] = (0, 0)
-    parent[(0, 8)] = (0, 6)
-    parent[(1, 8)] = (1, -6)
-    parent[(1, 0)] = (0, 0)
-    return parent
-
-
-ORDER = (8, 7, -7, 5, -5, 4, -4, 2, -2, 6, -6, 3, -3, 1, -1, 0)
+PARENT = {
+    (1, 7): (0, 7), (0, 8): (0, 7), (1, 8): (1, -7), (1, 6): (1, 5), (1, 3): (0, 3), (1, -5): (0, -5),
+    (1, -3): (1, -2), (0, -7): (0, -6), (0, 5): (0, 4), (0, 7): (0, 6), (1, -7): (0, -6), (1, -6): (0, -6),
+    (1, 5): (1, 4), (1, -2): (0, -2), (0, 3): (0, 2), (0, -5): (0, -4), (0, 6): (0, 4), (0, -3): (0, -2),
+    (1, 2): (0, 2), (1, 4): (0, 4), (0, -6): (0, -4), (1, -4): (0, -4), (0, 2): (0, 1), (1, 0): (0, 0),
+    (1, -1): (0, -1), (0, -2): (0, -1), (1, 1): (0, 1), (0, 4): (0, 0), (0, -4): (0, 0), (0, 1): (0, 0),
+    (0, -1): (0, 0),
+}
 PIECES = 5
 STRIDE = 289
 
 
 def kernel(
-    scale, image_hbm, refs_hbm, ids_hbm, ctf_hbm, noise_hbm, prior_hbm,
+    scale, image_hbm, refs_hbm, small_hbm,
     out_ref, occ_ref, evidence_ref,
-    image_ref, refs_ref, ids_ref, ctf_ref, noise_ref, prior_ref,
-    x_ref, xr_ref, w_ref, s_ref, score_ref, stats_ref, gath_ref, back_ref, y_ref, t_ref, den_ref, l_ref, r_ref,
+    image_ref, refs_ref, small_ref,
+    x_ref, xr_ref, w_ref, s_ref, even_ref, odd_ref, stats_ref, gath_ref, back_ref, y_ref, t_ref, den_ref, l_ref, r_ref,
     load_sem, gath_send, gath_recv, tree_send, tree_recv,
 ):
     images, _, cycles, harm = image_ref.shape
     classes = refs_ref.shape[0]
-    groups = ctf_ref.shape[1]
     count = folds(harm)
     rows = count * ROT
     depth = l_ref.shape[0]
@@ -113,14 +104,14 @@
     loads = [
         pltpu.make_async_copy(source, target, load_sem.at[n])
         for n, (source, target) in enumerate(
-            [(ids_hbm, ids_ref), (ctf_hbm, ctf_ref), (noise_hbm, noise_ref), (prior_hbm, prior_ref), (refs_hbm, refs_ref)]
+            [(small_hbm, small_ref), (refs_hbm, refs_ref)]
             + [(image_hbm.at[pl.ds(n * piece, piece)], image_ref.at[pl.ds(n * piece, piece)]) for n in range(PIECES)]
         )
     ]
     for load in loads:
         load.start()
 
-    parent = reduction_tree()
+    parent = PARENT
     index = {node: n for n, node in enumerate(parent)}
     children = {node: [other for other in parent if parent[other] == node] for node in [*parent, (0, 0)]}
     moves = {((parent[node][0] - node[0]) % 2, (parent[node][1] - node[1]) % depth) for node in parent}
@@ -141,11 +132,11 @@
     clear(x_ref, images, 8)
     clear(xr_ref, 2 * classes, 8)
 
-    for load in loads[:4]:
-        load.wait()
-    onehot = (iota((groups, images), 0) == ids_ref[...]).astype(F32)
-    ctf = jnp.dot(ctf_ref[...], onehot, precision=HP, preferred_element_type=F32)
-    noise = column(noise_ref[...])
+    loads[0].wait()
+    ids = small_ref[cycles : cycles + 1, :images].astype(jnp.int32)
+    onehot = (iota((LANES, images), 0) == ids).astype(F32)
+    ctf = jnp.dot(small_ref[:cycles], onehot, precision=HP, preferred_element_type=F32)
+    noise = column(small_ref[cycles + 1 : cycles + 2, :cycles])
     power = ctf * ctf / noise
     spread = (iota((cycles, LANES), 1) % SIDE == iota((cycles, LANES), 0)).astype(F32)
     weight = lax.dot_general(ctf / noise, spread, TN, precision=HP, preferred_element_type=F32)
@@ -155,7 +146,7 @@
     pick = ((row // 8) * share + row % 8 == iota(shape, 1)) & (row % 8 < share)
     by_dest = jnp.dot(pick.astype(F32), power, precision=HP, preferred_element_type=F32)
     by_dest = by_dest + (iota(by_dest.shape, 0) % 8 == share).astype(F32)
-    log_prior = column(jnp.log(prior_ref[...]))
+    log_prior = column(jnp.log(small_ref[cycles + 2 : cycles + 3, :classes]))
 
     eye = (iota((harm, harm), 0) == iota((harm, harm), 1)).astype(BF16)
     gap = jnp.zeros((SIDE - cycles, harm), BF16)
@@ -166,7 +157,7 @@
         ref[pl.ds(at0 * STRIDE, harm), :] = turned[:, :LANES]
         ref[pl.ds(at1 * STRIDE, harm), :] = turned[:, LANES:]
 
-    loads[4].wait()
+    loads[1].wait()
 
     @pl.loop(0, classes, unroll=8)
     def _(c):
@@ -174,7 +165,7 @@
         turn((real, imag), (imag, -real), xr_ref, c, classes + c)
 
     for n in range(PIECES):
-        loads[5 + n].wait()
+        loads[2 + n].wait()
 
         @pl.loop(0, piece // 2, unroll=8)
         def _(pair):
@@ -191,12 +182,13 @@
             w_ref[b, :, a * LANES : (a + 1) * LANES] = x_part
             image_parts.append(x_part)
             ref_parts.append(r_part.astype(BF16))
-        s_ref[b] = lax.dot_general(
+        product = lax.dot_general(
+            jnp.concatenate(image_parts, axis=1),
             jnp.concatenate(ref_parts, axis=1),
-            jnp.concatenate(image_parts, axis=1),
             NT,
             preferred_element_type=F32,
         )
+        s_ref[b] = product.T
         return squares
 
     squares = lax.fori_loop(0, ROT, one_residue, jnp.zeros((classes, LANES), F32), unroll=12)
@@ -207,20 +199,24 @@
     even = [real[0]] + [real[b] + real[ROT - b] for b in range(1, HALF)] + [real[HALF]]
     odd = [None] + [imag[b] - imag[ROT - b] for b in range(1, HALF)]
     cosines, sines = half_transform(even, odd)
-    peak = None
+    score = [None] * ROT
     for k in range(HALF + 1):
         centre = cosines[k] + base
-        made = [(k, centre)] if sines[k] is None else [(k, centre + sines[k]), (ROT - k, centre - sines[k])]
-        for at, value in made:
-            score_ref[at] = value
-            peak = value if peak is None else jnp.maximum(peak, value)
+        if sines[k] is None:
+            score[k] = centre
+        else:
+            score[k], score[ROT - k] = centre + sines[k], centre - sines[k]
+    peak = score[0]
+    for k in range(1, ROT):
+        peak = jnp.maximum(peak, score[k])
     peak = jnp.max(peak, axis=0, keepdims=True)
-    total = jnp.zeros((classes, images), F32)
-    for k in range(ROT):
-        total = total + jnp.exp(score_ref[k] - peak)
+    shifted = [jnp.exp(value - peak) for value in score]
+    mass = shifted[0]
+    for k in range(1, ROT):
+        mass = mass + shifted[k]
     stats_ref[...] = jnp.zeros(stats_ref.shape, F32)
     stats_ref[0:1, 0:images] = peak
-    stats_ref[1:2, 0:images] = jnp.sum(total, axis=0, keepdims=True)
+    stats_ref[1:2, 0:images] = jnp.sum(mass, axis=0, keepdims=True)
 
     pl.semaphore_wait(barrier, len(peers) + n_cls - 1)
     sends = []
@@ -235,26 +231,32 @@
         )
         copy.start()
         sends.append(copy)
+
+    even = [shifted[0]] + [shifted[k] + shifted[ROT - k] for k in range(1, HALF)] + [shifted[HALF]]
+    odd = [None] + [shifted[k] - shifted[ROT - k] for k in range(1, HALF)]
+    cosines, sines = half_transform(even, odd)
+    for b in range(HALF + 1):
+        even_ref[b] = cosines[b]
+        if sines[b] is not None:
+            odd_ref[b] = sines[b]
+
     for copy in sends:
         copy.wait_recv()
     parts = [stats_ref[...]] + [gath_ref[j] for j in range(1, n_cls)]
-    peak = parts[0][0:1, :images]
+    top = parts[0][0:1, :images]
     for part in parts[1:]:
-        peak = jnp.maximum(peak, part[0:1, :images])
+        top = jnp.maximum(top, part[0:1, :images])
     total = jnp.zeros((1, images), F32)
     for part in parts:
-        total = total + part[1:2, :images] * jnp.exp(part[0:1, :images] - peak)
-    evidence = peak + jnp.log(total)
+        total = total + part[1:2, :images] * jnp.exp(part[0:1, :images] - top)
+    evidence = top + jnp.log(total)
     evidence_ref[...] = evidence
 
-    posterior = [jnp.exp(score_ref[k] - evidence) for k in range(ROT)]
-    even = [posterior[0]] + [posterior[k] + posterior[ROT - k] for k in range(1, HALF)] + [posterior[HALF]]
-    odd = [None] + [posterior[k] - posterior[ROT - k] for k in range(1, HALF)]
-    cosines, sines = half_transform(even, odd)
-    mass = cosines[0]
+    factor = jnp.exp(peak - evidence)
+    mass = mass * factor
     for b in range(HALF + 1):
-        real = cosines[b].astype(BF16)
-        imag = jnp.zeros((classes, images), BF16) if sines[b] is None else sines[b].astype(BF16)
+        real = (even_ref[b] * factor).astype(BF16)
+        imag = jnp.zeros((classes, images), BF16) if sines[b] is None else (odd_ref[b] * factor).astype(BF16)
         back_ref[b] = jnp.concatenate([real, imag], axis=0)
         if 0 < b < HALF:
             back_ref[ROT - b] = jnp.concatenate([real, -imag], axis=0)
@@ -290,22 +292,7 @@
             device_id_type=MESH,
         )
 
-    def send(node):
-        towards(node, l_ref.at[at_z(-node[1]), at_x(node[0])]).start()
-
-    def gathered(node):
-        value = l_ref[at_z(-node[1]), at_x(node[0])]
-        for child in children[node]:
-            towards(child, l_ref.at[0, 0]).wait_recv()
-            value = value + r_ref[index[child]]
-        return value
-
-    def pass_on(node):
-        l_ref[at_z(-node[1]), at_x(node[0])] = gathered(node)
-        send(node)
-
-    for oz in ORDER:
-        dest = at_z(-oz)
+    def assemble(dest):
         for p in range(2):
             for j in range(share):
                 first = p * SIDE + dest * share + j
@@ -315,11 +302,23 @@
                         h, pl.ds(first, classes, stride=LANES), :
                     ]
             l_ref[dest, p, blocks * classes :, :] = den_ref[pl.ds(pl.multiple_of(dest * 8, 8), 8), :]
-        for ox in (0, 1):
-            if (ox, oz) in parent and not children[(ox, oz)]:
-                send((ox, oz))
-    for node in ((1, 6), (1, -6), (1, 3), (1, -3), (0, 6), (0, -6), (0, 3), (0, -3), (0, 1), (0, -1)):
-        pass_on(node)
+
+    def gathered(node):
+        value = l_ref[at_z(-node[1]), at_x(node[0])]
+        for child in children[node]:
+            towards(child, l_ref.at[0, 0]).wait_recv()
+            value = value + r_ref[index[child]]
+        return value
+
+    assembled = []
+    for node in parent:
+        place = at_z(-node[1]), at_x(node[0])
+        if node[1] not in assembled:
+            assemble(place[0])
+            assembled.append(node[1])
+        if children[node]:
+            l_ref[place] = gathered(node)
+        towards(node, l_ref.at[place]).start()
     mine = gathered((0, 0))
     tail = mine[blocks * classes :, :]
     occ_ref[...] = tail[share : share + 1, 0:classes] * scale
@@ -344,10 +343,17 @@
     rows = count * ROT
     width = cycles // depth * harm
     chunk = width // LANES * classes + 8
-    nodes = len(reduction_tree())
-    args = (
-        images, references, group_ids.reshape(1, -1), ctf_rows.T, noise_var.reshape(1, -1), class_prior.reshape(1, -1)
+    nodes = len(PARENT)
+    def fitted(rows, above):
+        return jnp.pad(rows, ((above, cycles + 8 - above - rows.shape[0]), (0, LANES - rows.shape[1])))
+
+    small = (
+        fitted(ctf_rows.T, 0)
+        + fitted(group_ids.astype(F32).reshape(1, -1), cycles)
+        + fitted(noise_var.reshape(1, -1), cycles + 1)
+        + fitted(class_prior.reshape(1, -1), cycles + 2)
     )
+    args = (images, references, small)
     new_references, occupancy, evidence = pl.pallas_call(
         functools.partial(kernel, classes * n_cls / (img_count * n_dp)),
         out_shape=[
@@ -355,7 +361,7 @@
             jax.ShapeDtypeStruct((1, classes), F32),
             jax.ShapeDtypeStruct((1, img_count), F32),
         ],
-        in_specs=[pl.BlockSpec(memory_space=pl.ANY)] * len(args),
+        in_specs=[pl.BlockSpec(memory_space=pltpu.HBM)] * len(args),
         out_specs=[pl.BlockSpec(memory_space=pltpu.VMEM)] * 3,
         scratch_shapes=[
             *[pltpu.VMEM(arg.shape, arg.dtype) for arg in args],
@@ -363,7 +369,8 @@
             pltpu.VMEM((2 * classes * STRIDE, LANES), F32),
             pltpu.VMEM((ROT, img_count, count * LANES), BF16),
             pltpu.VMEM((ROT, 2 * classes, img_count), F32),
-            pltpu.VMEM((ROT, classes, img_count), F32),
+            pltpu.VMEM((HALF + 1, classes, img_count), F32),
+            pltpu.VMEM((HALF + 1, classes, img_count), F32),
             pltpu.VMEM((8, LANES), F32),
             pltpu.VMEM((n_cls, 8, LANES), F32),
             pltpu.VMEM((ROT, 2 * classes, img_count), BF16),
@@ -372,14 +379,14 @@
             pltpu.VMEM((depth * 8, LANES), F32),
             pltpu.VMEM((depth, 2, chunk, LANES), F32),
             pltpu.VMEM((nodes, chunk, LANES), F32),
-            pltpu.SemaphoreType.DMA((5 + PIECES,)),
+            pltpu.SemaphoreType.DMA((2 + PIECES,)),
             pltpu.SemaphoreType.DMA((n_cls,)),
             pltpu.SemaphoreType.DMA((n_cls,)),
             pltpu.SemaphoreType.DMA((nodes,)),
             pltpu.SemaphoreType.DMA((nodes,)),
         ],
         compiler_params=pltpu.CompilerParams(
-            collective_id=0, has_side_effects=True, vmem_limit_bytes=56 * 2**20
+            collective_id=0, has_side_effects=True, vmem_limit_bytes=107 * 2**19
         ),
     )(*args)
     return new_references, occupancy.reshape(-1), evidence.reshape(-1)

time: 60.5 us -> 51.7 us (0.85)
  the two profiles are of different devices: /device:TPU:1 before, /device:TPU:8 now
where the time goes in v3:
time: 51.7 us; the launch traced here: 51.5 us
  Pallas kernels  47.7 us (92%)
  local copies, waits for them, and re-layouts  1.64 us (3%)
  other arithmetic  1.44 us (3%)
  between operations  0.64 us (1%)
    pallas_call x1, Pallas kernels, shards(): pl.pallas_call(functools.partial(kernel, classes * n_cls / (img_count * n...  47.7 us
    unnamed x3, local copies, waits for them, and re-layouts  1.64 us

profile of v3, /device:TPU:8, one launch (start us, length us, event | category | flops | bytes accessed | tf_op | source)
XLA Modules:
  0.0 51.5 jit_solution(9830500283063391102)
XLA Ops:
  0.6 0.7 %convert_bitcast_fusion = f32[1,80]{1,0:T(1,128)S(1)} fusion(s32[80]{0:T(128)} %param.9), kind=kLoop, calls=%fused_computation.1 | loop fusion | flops 80 | bytes 640 | tf_op jit(solution)/shard_map/reshape | solution.py:352
  1.3 0.8 %pad_add_fusion.small_hbm = f32[56,128]{1,0:T(8,128)S(1)} fusion(f32[1,16]{1,0:T(1,128)} %bitcast.10, f32[1,48]{1,0:T(1,128)} %bitcast.11, f32[1,80]{1,0:T(1,128)S(1)} %convert_bitcast_fusion, f32[48,64]{1,0:T(8,128)} %bitcast.9), kind=kLoop, calls=%fused_computation | loop fusion | flops 21504 | bytes 41536 | tf_op jit(solution)/shard_map/add | solution.py:351
  2.1 47.7 %shard_map.85 = (f32[16,768]{1,0:T(8,128)S(1)}, f32[1,16]{1,0:T(1,128)S(1)}, f32[1,80]{1,0:T(1,128)S(1)}) custom-call(bf16[80,2,48,256]{3,2,1,0:T(8,128)(2,1)} %image_hbm.1, bf16[16,2,48,256]{3,2,1,0:T(8,128)(2,1)} %refs_hbm.1, f32[56,128]{1,0:T(8,128)S(1)} %pad_add_fusion.small_hbm), custom_call_target="tpu_custom_call" | custom-call | tf_op jit(solution)/shard_map/pallas_call | solution.py:357
  49.8 0.6 %copy.12 = f32[16,768]{1,0:T(8,128)} copy(f32[16,768]{1,0:T(8,128)S(1)} %get-tuple-element.12) | data formatting | bytes 98304
  50.4 0.5 copy.13
  51.0 0.5 copy.14

commit v4 on v3

--- a/solution.py
+++ b/solution.py
@@ -101,6 +101,21 @@
     def at_x(step):
         return (x + step) % 2
 
+    ring = n_cls // 4
+
+    def beside(j):
+        return (
+            (cls // (2 * ring) + j // (2 * ring)) % 2 * (2 * ring)
+            + (cls // 2 % ring + j // 2 % ring) % ring * 2
+            + (cls + j) % 2
+        )
+
+    def distance(j):
+        y = j // 2 % ring
+        return 2 * (j // (2 * ring)) + min(y, ring - y) + 0.1 * (j % 2)
+
+    around = sorted(range(1, n_cls), key=distance, reverse=True)
+
     loads = [
         pltpu.make_async_copy(source, target, load_sem.at[n])
         for n, (source, target) in enumerate(
@@ -121,8 +136,8 @@
         pl.semaphore_signal(
             barrier, inc=1, device_id={"dp": at_x(ox) * depth + at_z(oz), "cls": cls}, device_id_type=MESH
         )
-    for j in range(1, n_cls):
-        pl.semaphore_signal(barrier, inc=1, device_id={"dp": dp, "cls": (cls + j) % n_cls}, device_id_type=MESH)
+    for j in around:
+        pl.semaphore_signal(barrier, inc=1, device_id={"dp": dp, "cls": beside(j)}, device_id_type=MESH)
 
     def clear(ref, total, unroll):
         @pl.loop(0, total, unroll=unroll)
@@ -159,7 +174,7 @@
 
     loads[1].wait()
 
-    @pl.loop(0, classes, unroll=8)
+    @pl.loop(0, classes, unroll=16)
     def _(c):
         real, imag = refs_ref[c, 0], refs_ref[c, 1]
         turn((real, imag), (imag, -real), xr_ref, c, classes + c)
@@ -191,7 +206,7 @@
         s_ref[b] = product.T
         return squares
 
-    squares = lax.fori_loop(0, ROT, one_residue, jnp.zeros((classes, LANES), F32), unroll=12)
+    squares = lax.fori_loop(0, ROT, one_residue, jnp.zeros((classes, LANES), F32), unroll=36)
     model = lax.dot_general(squares, power_lanes, NT, precision=HP, preferred_element_type=F32)
     base = log_prior - 0.5 * model
     real = [s_ref[b, :classes] for b in range(ROT)]
@@ -220,13 +235,13 @@
 
     pl.semaphore_wait(barrier, len(peers) + n_cls - 1)
     sends = []
-    for j in range(1, n_cls):
+    for j in around:
         copy = pltpu.make_async_remote_copy(
             src_ref=stats_ref,
             dst_ref=gath_ref.at[j],
             send_sem=gath_send.at[j],
             recv_sem=gath_recv.at[j],
-            device_id={"dp": dp, "cls": (cls + j) % n_cls},
+            device_id={"dp": dp, "cls": beside(j)},
             device_id_type=MESH,
         )
         copy.start()
@@ -265,7 +280,7 @@
 
     sign = jnp.where(iota((classes, LANES), 1) < SIDE, -1.0, 1.0)
 
-    @pl.loop(0, ROT, unroll=12)
+    @pl.loop(0, ROT, unroll=36)
     def _(b):
         both = jnp.dot(back_ref[b], w_ref[b], preferred_element_type=F32)
         for a in range(count):
@@ -274,7 +289,7 @@
                 part[classes:], SIDE, 1
             )
 
-    @pl.loop(0, classes, unroll=4)
+    @pl.loop(0, classes, unroll=16)
     def _(c):
         for h in range(halves):
             t_ref[h, pl.ds(pl.multiple_of(c * LANES, LANES), LANES), :] = y_ref[
@@ -349,7 +364,7 @@
 
     small = (
         fitted(ctf_rows.T, 0)
-        + fitted(group_ids.astype(F32).reshape(1, -1), cycles)
+        + fitted(group_ids.reshape(1, -1), cycles).astype(F32)
         + fitted(noise_var.reshape(1, -1), cycles + 1)
         + fitted(class_prior.reshape(1, -1), cycles + 2)
     )

time: 51.7 us -> 48.7 us (0.942)
  the two profiles are of different devices: /device:TPU:8 before, /device:TPU:2 now
where the time goes in v4:
time: 48.7 us; the launch traced here: 48.5 us
  Pallas kernels  45.4 us (93%)
  local copies, waits for them, and re-layouts  1.64 us (3%)
  other arithmetic  0.8 us (2%)
  between operations  0.64 us (1%)
    pallas_call x1, Pallas kernels, shards(): pl.pallas_call(functools.partial(kernel, classes * n_cls / (img_count * n...  45.4 us
    unnamed x3, local copies, waits for them, and re-layouts  1.64 us

profile of v4, /device:TPU:2, one launch (start us, length us, event | category | flops | bytes accessed | tf_op | source)
XLA Modules:
  0.0 48.5 jit_solution(7627402988915529489)
XLA Ops:
  0.6 0.8 %pad_add_fusion.small_hbm = f32[56,128]{1,0:T(8,128)S(1)} fusion(f32[1,16]{1,0:T(1,128)} %bitcast.9, f32[1,48]{1,0:T(1,128)} %bitcast.10, s32[1,80]{1,0:T(1,128)} %bitcast.11, f32[48,64]{1,0:T(8,128)} %bitcast.8), kind=kLoop, calls=%fused_computation | loop fusion | flops 28672 | bytes 41536 | tf_op jit(solution)/shard_map/add | solution.py:366
  1.4 45.4 %shard_map.85 = (f32[16,768]{1,0:T(8,128)S(1)}, f32[1,16]{1,0:T(1,128)S(1)}, f32[1,80]{1,0:T(1,128)S(1)}) custom-call(bf16[80,2,48,256]{3,2,1,0:T(8,128)(2,1)} %image_hbm.1, bf16[16,2,48,256]{3,2,1,0:T(8,128)(2,1)} %refs_hbm.1, f32[56,128]{1,0:T(8,128)S(1)} %pad_add_fusion.small_hbm), custom_call_target="tpu_custom_call" | custom-call | tf_op jit(solution)/shard_map/pallas_call | solution.py:372
  46.8 0.6 %copy.12 = f32[16,768]{1,0:T(8,128)} copy(f32[16,768]{1,0:T(8,128)S(1)} %get-tuple-element.12) | data formatting | bytes 98304
  47.4 0.5 %copy.13 = f32[16]{0:T(128)} copy(f32[16]{0:T(128)S(1)} %bitcast.7) | data formatting | bytes 128
  48.0 0.5 %copy.14 = f32[80]{0:T(128)} copy(f32[80]{0:T(128)S(1)} %bitcast.6) | data formatting | bytes 640

commit v5 on v4

--- a/solution.py
+++ b/solution.py
@@ -70,7 +70,7 @@
     (1, -1): (0, -1), (0, -2): (0, -1), (1, 1): (0, 1), (0, 4): (0, 0), (0, -4): (0, 0), (0, 1): (0, 0),
     (0, -1): (0, 0),
 }
-PIECES = 5
+PIECES = 2
 STRIDE = 289
 
 
@@ -182,7 +182,7 @@
     for n in range(PIECES):
         loads[2 + n].wait()
 
-        @pl.loop(0, piece // 2, unroll=8)
+        @pl.loop(0, piece // 2, unroll=20)
         def _(pair):
             i = n * piece + pair * 2
             turn((image_ref[i, 0], image_ref[i, 1]), (image_ref[i + 1, 0], image_ref[i + 1, 1]), x_ref, i, i + 1)

time: 48.7 us -> 48.3 us (level)
  no operation moved by 1% of the time
where the time goes in v5:
time: 48.3 us; the launch traced here: 48.1 us
  Pallas kernels  45 us (93%)
  local copies, waits for them, and re-layouts  1.64 us (3%)
  other arithmetic  0.8 us (2%)
  between operations  0.64 us (1%)
    pallas_call x1, Pallas kernels, shards(): pl.pallas_call(functools.partial(kernel, classes * n_cls / (img_count * n...  45 us
    unnamed x3, local copies, waits for them, and re-layouts  1.64 us

profile of v5, /device:TPU:2, one launch (start us, length us, event | category | flops | bytes accessed | tf_op | source)
XLA Modules:
  0.0 48.1 jit_solution(17461417437906232652)
XLA Ops:
  0.6 0.8 %pad_add_fusion.small_hbm = f32[56,128]{1,0:T(8,128)S(1)} fusion(f32[1,16]{1,0:T(1,128)} %bitcast.9, f32[1,48]{1,0:T(1,128)} %bitcast.10, s32[1,80]{1,0:T(1,128)} %bitcast.11, f32[48,64]{1,0:T(8,128)} %bitcast.8), kind=kLoop, calls=%fused_computation | loop fusion | flops 28672 | bytes 41536 | tf_op jit(solution)/shard_map/add | solution.py:366
  1.4 45.0 %shard_map.85 = (f32[16,768]{1,0:T(8,128)S(1)}, f32[1,16]{1,0:T(1,128)S(1)}, f32[1,80]{1,0:T(1,128)S(1)}) custom-call(bf16[80,2,48,256]{3,2,1,0:T(8,128)(2,1)} %image_hbm.1, bf16[16,2,48,256]{3,2,1,0:T(8,128)(2,1)} %refs_hbm.1, f32[56,128]{1,0:T(8,128)S(1)} %pad_add_fusion.small_hbm), custom_call_target="tpu_custom_call" | custom-call | tf_op jit(solution)/shard_map/pallas_call | solution.py:372
  46.5 0.6 %copy.12 = f32[16,768]{1,0:T(8,128)} copy(f32[16,768]{1,0:T(8,128)S(1)} %get-tuple-element.12) | data formatting | bytes 98304
  47.1 0.5 %copy.13 = f32[16]{0:T(128)} copy(f32[16]{0:T(128)S(1)} %bitcast.7) | data formatting | bytes 128
  47.6 0.5 %copy.14 = f32[80]{0:T(128)} copy(f32[80]{0:T(128)S(1)} %bitcast.6) | data formatting | bytes 640

commit v6 on v5

--- a/solution.py
+++ b/solution.py
@@ -182,10 +182,14 @@
     for n in range(PIECES):
         loads[2 + n].wait()
 
-        @pl.loop(0, piece // 2, unroll=20)
-        def _(pair):
-            i = n * piece + pair * 2
-            turn((image_ref[i, 0], image_ref[i, 1]), (image_ref[i + 1, 0], image_ref[i + 1, 1]), x_ref, i, i + 1)
+        @pl.loop(0, piece // 10, unroll=piece // 10)
+        def _(group):
+            i = n * piece + group * 10
+            for at in (i, i + 2):
+                turn((image_ref[at, 0], image_ref[at, 1]), (image_ref[at + 1, 0], image_ref[at + 1, 1]), x_ref, at, at + 1)
+            for step in range(4, 10):
+                block = jnp.concatenate([image_ref[i + step, 0], gap, image_ref[i + step, 1], gap], axis=0)
+                x_ref[pl.ds((i + step) * STRIDE, harm), :] = block.astype(F32).T
 
     def one_residue(b, squares):
         image_parts, ref_parts = [], []

time: 48.3 us -> 47.6 us (0.986)
  Pallas kernels: 45 us -> 44.3 us
    pallas_call x1, Pallas kernels: 45 us -> 44.3 us  [shards(): pl.pallas_call(functools.partial(kernel, classes * n_cls / (img_count * n...]
where the time goes in v6:
time: 47.6 us; the launch traced here: 47.4 us
  Pallas kernels  44.3 us (93%)
  local copies, waits for them, and re-layouts  1.64 us (3%)
  other arithmetic  0.8 us (2%)
  between operations  0.64 us (1%)
    pallas_call x1, Pallas kernels, shards(): pl.pallas_call(functools.partial(kernel, classes * n_cls / (img_count * n...  44.3 us
    unnamed x3, local copies, waits for them, and re-layouts  1.64 us

profile of v6, /device:TPU:2, one launch (start us, length us, event | category | flops | bytes accessed | tf_op | source)
XLA Modules:
  0.0 47.4 jit_solution(10813603442287315773)
XLA Ops:
  0.6 0.8 %pad_add_fusion.small_hbm = f32[56,128]{1,0:T(8,128)S(1)} fusion(f32[1,16]{1,0:T(1,128)} %bitcast.9, f32[1,48]{1,0:T(1,128)} %bitcast.10, s32[1,80]{1,0:T(1,128)} %bitcast.11, f32[48,64]{1,0:T(8,128)} %bitcast.8), kind=kLoop, calls=%fused_computation | loop fusion | flops 28672 | bytes 41536 | tf_op jit(solution)/shard_map/add | solution.py:370
  1.4 44.3 %shard_map.85 = (f32[16,768]{1,0:T(8,128)S(1)}, f32[1,16]{1,0:T(1,128)S(1)}, f32[1,80]{1,0:T(1,128)S(1)}) custom-call(bf16[80,2,48,256]{3,2,1,0:T(8,128)(2,1)} %image_hbm.1, bf16[16,2,48,256]{3,2,1,0:T(8,128)(2,1)} %refs_hbm.1, f32[56,128]{1,0:T(8,128)S(1)} %pad_add_fusion.small_hbm), custom_call_target="tpu_custom_call" | custom-call | tf_op jit(solution)/shard_map/pallas_call | solution.py:376
  45.7 0.6 %copy.12 = f32[16,768]{1,0:T(8,128)} copy(f32[16,768]{1,0:T(8,128)S(1)} %get-tuple-element.12) | data formatting | bytes 98304
  46.4 0.5 %copy.13 = f32[16]{0:T(128)} copy(f32[16]{0:T(128)S(1)} %bitcast.7) | data formatting | bytes 128
  46.9 0.5 %copy.14 = f32[80]{0:T(128)} copy(f32[80]{0:T(128)S(1)} %bitcast.6) | data formatting | bytes 640
